TPU v7x, 256 devices: a whole 4x4x8 slice. The times are simulated.
256 devices in a mesh: pitch: 32 (over y, z), span: 8 (over x, core).
Axes of the slice: x: 4, y: 4, z: 8, core: 2. Of those that a mesh axis runs over, the one named last changes fastest.
Arguments:
- fields: float32 [5, 256, 65536], P(None, 'span', 'pitch'), may hold values from -10 to 10
- diffusivity: float32 [256, 65536], P('span', 'pitch'), may hold values from 0.1 to 0.24
- mixing: float32 [256, 256], replicated, may hold values from -0.375 to 0.375
- cond_gain: float32 [5], replicated, may hold values from -1 to 1
- advection: float32 [5, 2], replicated, may hold values from -0.35 to 0.35
- parcels: float32 [16, 2097152], P(None, ('pitch', 'span')), may hold values from -6 to 6
- cell: int32 [2097152], P(('pitch', 'span')), may hold values from 0 to 65535
- couple: float32 [5, 16], replicated, may hold values from -1.5 to 1.5
- relax: float32 [16], replicated, may hold values from 0.02 to 0.9
- drag: float32 [16, 5], replicated, may hold values from -2.5 to 2.5
- counts: int32 [8192], P(('pitch', 'span')), may hold values from 0 to 512, as said below
Outputs:
- new_fields: float32 [5, 256, 65536], P(None, 'span', 'pitch')
- arrived: float32 [16, 4194304], P(None, ('pitch', 'span'))
Inputs may be any that keep to these rules, and one draw needn't show every extreme that they name: `counts`: each device's entries sum to 8192; one pitch index, drawn from the seed, gets exactly 512 parcels from every device.
All inputs are finite; a program needn't handle non-finite values.
Results may differ from a plain program's by a relative error of at most 0.000086.
Values sent between devices are 32-bit elements; how exact they have to be, the bound alone decides.
A program may use at most 128 MiB of HBM per device.

v0:
```python
import jax
import jax.numpy as jnp
from jax import lax
from jax.sharding import PartitionSpec as P

SUBSTEPS = 2


def padded_2(block, sides, width):
    for axis, dim in sides:
        count = lax.axis_size(axis)
        forward = [(i, i + 1) for i in range(count - 1)]
        backward = [(target, source) for source, target in forward]
        low = lax.ppermute(
            lax.slice_in_dim(block, block.shape[dim] - width, None, axis=dim), axis, forward
        )
        high = lax.ppermute(lax.slice_in_dim(block, 0, width, axis=dim), axis, backward)
        block = jnp.concatenate([low, block, high], axis=dim)
    return block


def advance(padded, source, nu, advection):
    centre = padded[:, 1:-1, 1:-1]
    upper = padded[:, 2:, 1:-1]
    lower = padded[:, :-2, 1:-1]
    right = padded[:, 1:-1, 2:]
    left_side = padded[:, 1:-1, :-2]
    radial = advection[:, 0][:, None, None]
    across = advection[:, 1][:, None, None]
    return (
        centre
        + 0.25 * source
        + radial * (upper - lower)
        + across * (right - left_side)
        + nu * (upper + lower + right + left_side - 4.0 * centre)
    )


def local(
    fields, diffusivity, mixing, cond_gain, advection, parcels, cell, couple, relax, drag, counts
):
    high = lax.Precision.HIGHEST
    nfield, rows, cols = fields.shape
    pitch_count = lax.axis_size("pitch")
    span_me = lax.axis_index("span")
    proj = jnp.dot(couple, parcels, precision=high, preferred_element_type=jnp.float32)
    deposit = (
        jnp.zeros((nfield, rows * cols), jnp.float32)
        .at[:, cell]
        .add(proj)
        .reshape(nfield, rows, cols)
    )
    profile = jnp.mean(fields, axis=2)
    whole = lax.all_gather(profile, "span", axis=1, tiled=True)
    my_rows = lax.dynamic_slice_in_dim(mixing, span_me * rows, rows, 0)
    corr = jnp.einsum("fs,rs->fr", whole, my_rows, precision=high)
    rate = jax.nn.softplus(fields[0] + corr[0][:, None]) * (
        1.0 + jnp.tanh(fields[1] + corr[1][:, None])
    )
    source = cond_gain[:, None, None] * rate[None] - 0.5 * corr[:, :, None] + deposit
    state = fields
    for step in range(SUBSTEPS):
        padded = padded_2(state, (("pitch", 2), ("span", 1)), 1)
        state = advance(padded, source, diffusivity[None], advection)
    local_fluid = fields.reshape(nfield, rows * cols)[:, cell]
    moved = (1.0 - relax[:, None]) * parcels + jnp.dot(
        drag, local_fluid, precision=high, preferred_element_type=jnp.float32
    )
    capacity = 2 * parcels.shape[1] // pitch_count
    offsets = jnp.cumsum(counts) - counts
    slot = jnp.arange(capacity, dtype=jnp.int32)
    valid = slot[None, :] < counts[:, None]
    index = jnp.where(valid, offsets[:, None] + slot[None, :], 0)
    outgoing = jnp.where(valid[None], moved[:, index], 0.0)
    incoming = lax.all_to_all(outgoing, "pitch", split_axis=1, concat_axis=1, tiled=True)
    arrived = incoming.reshape(parcels.shape[0], pitch_count * capacity)
    return (state, arrived)


def solution(mesh):
    return jax.shard_map(
        local,
        mesh=mesh,
        in_specs=(
            P(None, "span", "pitch"),
            P("span", "pitch"),
            P(),
            P(),
            P(),
            P(None, ("pitch", "span")),
            P(("pitch", "span")),
            P(),
            P(),
            P(),
            P(("pitch", "span")),
        ),
        out_specs=(P(None, "span", "pitch"), P(None, ("pitch", "span"))),
        check_vma=False,
    )
```

profile of v0, /device:TPU:28, one launch (start us, length us, event | category | flops | bytes accessed | tf_op | source)
XLA Modules:
  0.0 289.1 jit_solution(18354701713976687625)
XLA Ops:
  0.6 0.0 copy-start
  0.6 1.1 fusion.12
  1.7 7.9 %collective-permute-start.1 = (f32[5,32,1]{2,1,0:T(8,128)S(1)}, f32[5,32,1]{2,1,0:T(8,128)S(1)}, u32[]{:S(2)}, u32[]{:S(2)}) collective-permute-start(f32[5,32,1]{2,1,0:T(8,128)S(1)} %get-tuple-element.9), channel_id=1, source_target_pairs={{8,0},{16,8},{24,16},{32,24},{40,32},{48,40},{56,48},{64,56},{72,6... | collective-permute-start | bytes 1928 | tf_op jit(solution)/shard_map/ppermute | solution.py:17
  9.7 0.0 copy-start.12
  9.7 0.0 copy-start.18
  9.7 1.9 collective-permute-start
  11.6 17.7 %copy.35 = f32[5,32,2048]{0,2,1:T(8,128)} copy(f32[5,32,2048]{2,1,0:T(8,128)} %param.11) | data formatting | bytes 2621440 | tf_op args[0]
  29.3 0.0 copy-done.12
  29.3 0.0 copy-done.18
  29.3 38.3 %gather_fusion = f32[8192,5]{1,0:T(8,128)} fusion(f32[5,65536]{0,1:T(8,128)} %bitcast.38, s32[8192]{0:T(1024)S(1)} %get-tuple-element.10), kind=kCustom, calls=%fused_computation | custom fusion | bytes 360448 | tf_op jit(solution)/shard_map/gather | solution.py:65
  67.7 0.0 copy-done.5
  67.7 0.0 copy-done.14
  67.7 5.5 %fusion.2 = f32[16,8192]{1,0:T(8,128)S(1)} fusion(f32[8192,5]{1,0:T(8,128)} %gather_fusion, f32[16,5]{0,1:T(8,128)S(1)} %copy-done.14, f32[16,8192]{1,0:T(8,128)S(1)} %copy-done.5, f32[16]{0:T(128)S(1)} %broadcast_subtract_fusion), kind=kOutput, calls=%fused_computation.6 | convolution fusion | flops 8126464 | bytes 1212800 | tf_op jit(solution)/shard_map/dot_general | solution.py:66
  73.2 0.0 copy-start.13
  73.2 2.7 copy.37
  75.8 0.0 copy-done.13
  75.8 0.1 iota_compare_fusion.1
  75.9 0.1 copy.36
  76.0 0.1 reduce-window.9
  76.1 0.1 reduce
  76.2 0.1 fusion.5
  76.3 56.6 %gather_fusion.1 = f32[16384,16]{1,0:T(8,128)} fusion(f32[16,8192]{0,1:T(8,128)} %copy.37, s32[16384]{0:T(1024)S(1)} %broadcast_clamp_fusion), kind=kCustom, calls=%fused_computation.1 | custom fusion | bytes 2162688 | tf_op jit(solution)/shard_map/gather | solution.py:74
  133.0 5.1 %copy.38 = f32[32,512,16]{1,2,0:T(8,128)S(1)} copy(f32[32,512,16]{2,1,0:T(8,128)} %bitcast.39) | data formatting | bytes 2097152 | tf_op jit(solution)/shard_map/gather | solution.py:74
  138.1 1.1 select_bitcast_fusion
  139.2 8.5 %all-to-all-start = ((f32[16,32,512]{2,0,1:T(8,128)}), f32[16,32,512]{2,0,1:T(8,128)}, u32[]{:S(2)}, u32[]{:S(2)}) async-start(f32[16,32,512]{2,0,1:T(8,128)} %select_bitcast_fusion), calls=%async_computation | async-start | bytes 2097152 | tf_op jit(solution)/shard_map/all_to_all | solution.py:75
  147.7 0.0 copy-start.15
  147.7 0.0 copy-done.2
  147.7 0.1 reduce_sum.9
  147.9 11.6 %all-gather = f32[8,32,5]{1,2,0:T(8,128)S(1)} all-gather(f32[1,32,5]{1,2,0:T(8,128)S(1)} %multiply_bitcast_fusion), channel_id=1, replica_groups=mesh['pitch'=32,'span'=8] {'span'}, dimensions={0}, use_global_device_ids=true | all-gather | bytes 5760 | tf_op jit(solution)/shard_map/all_gather | solution.py:54
  159.5 0.1 reshape.184
  159.6 0.0 copy-done
  159.6 0.1 broadcast_multiply_fusion
  159.7 0.3 fusion.4
  160.0 0.0 copy-done.15
  160.0 8.3 %fusion.13 = f32[8192,5]{1,0:T(8,128)} fusion(f32[16,8192]{1,0:T(8,128)S(1)} %copy-done.5, f32[5,16]{1,0:T(8,128)S(1)} %copy-done.15), kind=kOutput, calls=%fused_computation.43 | convolution fusion | flops 7864320 | bytes 688448 | tf_op jit(solution)/shard_map/dot_general | solution.py:46
  168.3 0.0 collective-permute-done.1
  168.3 0.0 collective-permute-done
  168.3 0.0 copy-start.9
  168.3 0.9 concatenate.32
  169.3 0.0 copy-done.7
  169.3 0.1 fusion.10
  169.4 3.6 %collective-permute-start.2 = (f32[5,1,2050]{2,1,0:T(1,128)S(1)}, f32[5,1,2050]{2,1,0:T(1,128)S(1)}, u32[]{:S(2)}, u32[]{:S(2)}) collective-permute-start(f32[5,1,2050]{2,1,0:T(1,128)S(1)} %get-tuple-element.5), channel_id=1, source_target_pairs={{1,0},{2,1},{3,2},{4,3},{5,4},{6,5},{7,6},{9,8},{10,9},{11,10},{12... | collective-permute-start | bytes 123008 | tf_op jit(solution)/shard_map/ppermute | solution.py:17
  173.0 2.1 collective-permute-start.3
  175.1 57.5 %scatter_custom_fusion = f32[5,65536]{0,1:T(8,128)} fusion(s32[8192]{0:T(1024)S(1)} %get-tuple-element.11, f32[8192,5]{1,0:T(8,128)} %fusion.13, f32[]{:T(128)} %constant.12.clone.1), kind=kCustom, calls=%fused_computation.3 | custom fusion | flops 40960 | bytes 1311232 | tf_op jit(solution)/shard_map/scatter-add | solution.py:50
  232.6 0.0 copy-start.16
  232.6 20.4 %copy.34 = f32[5,32,2048]{2,1,0:T(8,128)} copy(f32[5,32,2048]{0,2,1:T(8,128)} %bitcast.37) | data formatting | bytes 2621440 | tf_op jit(solution)/shard_map/reshape | solution.py:51
  253.0 0.0 collective-permute-done.2
  253.0 0.0 collective-permute-done.3
  253.1 4.0 %multiply_add_fusion.1 = f32[5,32,2048]{2,1,0:T(8,128)S(1)} fusion(f32[5,32,2048]{2,1,0:T(8,128)S(1)} %copy-done.2, f32[5,32,1]{2,1,0:T(8,128)S(1)} %copy-done.8, f32[5,32,1]{2,1,0:T(8,128)S(1)} %copy-done.10, f32[5,1,2050]{2,1,0:T(1,128)S(1)} %collective-permute-done.2, f32[5,32,2050]{2,1,0:T(8,128)} %copy-done.4, ...), kind=kLoop, calls=%fused_computation.16 | loop fusion | flops 7208960 | bytes 5852428 | tf_op jit(solution)/shard_map/add | solution.py:31
  257.1 0.1 fusion.11
  257.2 4.9 %collective-permute-start.5 = (f32[5,32,1]{2,1,0:T(8,128)S(1)}, f32[5,32,1]{2,1,0:T(8,128)S(1)}, u32[]{:S(2)}, u32[]{:S(2)}) collective-permute-start(f32[5,32,1]{2,1,0:T(8,128)S(1)} %get-tuple-element.7), channel_id=1, source_target_pairs={{8,0},{16,8},{24,16},{32,24},{40,32},{48,40},{56,48},{64,56},{72,6... | collective-permute-start | bytes 1928 | tf_op jit(solution)/shard_map/ppermute | solution.py:17
  262.0 0.0 copy-start.3
  262.0 2.1 collective-permute-start.4
  264.1 0.6 collective-permute-done.5
  264.7 6.4 %collective-permute-done.4 = f32[5,32,1]{2,1,0:T(8,128)S(1)} collective-permute-done((f32[5,32,1]{2,1,0:T(8,128)S(1)}, f32[5,32,1]{2,1,0:T(8,128)S(1)}, u32[]{:S(2)}, u32[]{:S(2)}) %collective-permute-start.4) | collective-permute-done | bytes 672 | tf_op jit(solution)/shard_map/ppermute | solution.py:14
  271.1 1.5 concatenate.37
  272.6 1.1 fusion.9
  273.8 2.9 %collective-permute-start.6 = (f32[5,1,2050]{2,1,0:T(1,128)S(1)}, f32[5,1,2050]{2,1,0:T(1,128)S(1)}, u32[]{:S(2)}, u32[]{:S(2)}) collective-permute-start(f32[5,1,2050]{2,1,0:T(1,128)S(1)} %get-tuple-element.3), channel_id=1, source_target_pairs={{1,0},{2,1},{3,2},{4,3},{5,4},{6,5},{7,6},{9,8},{10,9},{11,10},{12... | collective-permute-start | bytes 123008 | tf_op jit(solution)/shard_map/ppermute | solution.py:17
  276.7 1.9 collective-permute-start.7
  278.6 0.0 collective-permute-done.6
  278.6 3.4 %collective-permute-done.7 = f32[5,1,2050]{2,1,0:T(1,128)S(1)} collective-permute-done((f32[5,1,2050]{2,1,0:T(1,128)S(1)}, f32[5,1,2050]{2,1,0:T(1,128)S(1)}, u32[]{:S(2)}, u32[]{:S(2)}) %collective-permute-start.7) | collective-permute-done | bytes 41032 | tf_op jit(solution)/shard_map/ppermute | solution.py:14
  282.0 4.8 %multiply_add_fusion = f32[5,32,2048]{2,1,0:T(8,128)} fusion(f32[5,32,2048]{2,1,0:T(8,128)S(1)} %multiply_add_fusion.1, f32[5,32,1]{2,1,0:T(8,128)S(1)} %collective-permute-done.5, f32[5,32,1]{2,1,0:T(8,128)} %copy-done.11, f32[5,1,2050]{2,1,0:T(1,128)S(1)} %collective-permute-done.6, f32[5,32,2050]{2,1,0:T(8,128)} %concatenate.37, ...), kind=kLoop, calls=%fused_computation.15 | loop fusion | flops 7208960 | bytes 5852428 | tf_op jit(solution)/shard_map/add | solution.py:31
  286.8 0.0 all-to-all-done
  286.9 2.3 copy.41
  (30 shorter events, 0.1 us)
Async XLA Ops:
  0.6 158.9 %copy-start = (f32[256,256]{1,0:T(8,128)S(1)}, f32[256,256]{1,0:T(8,128)}, u32[]{:S(2)}) copy-start(f32[256,256]{1,0:T(8,128)} %param.13) | copy-start | bytes 786436
  1.7 166.6 %collective-permute-start.1 = (f32[5,32,1]{2,1,0:T(8,128)S(1)}, f32[5,32,1]{2,1,0:T(8,128)S(1)}, u32[]{:S(2)}, u32[]{:S(2)}) collective-permute-start(f32[5,32,1]{2,1,0:T(8,128)S(1)} %get-tuple-element.9), channel_id=1, source_target_pairs={{8,0},{16,8},{24,16},{32,24},{40,32},{48,40},{56,48},{64,56},{72,6... | collective-permute-start | bytes 1928 | tf_op jit(solution)/shard_map/ppermute | solution.py:17
  9.7 19.6 %copy-start.12 = (s32[8192]{0:T(1024)S(1)}, s32[8192]{0:T(1024)}, u32[]{:S(2)}) copy-start(s32[8192]{0:T(1024)} %param.17) | copy-start | bytes 98308
  9.7 19.7 %copy-start.18 = (f32[16]{0:T(128)S(1)}, f32[16]{0:T(128)}, u32[]{:S(2)}) copy-start(f32[16]{0:T(128)} %param.19) | copy-start | bytes 196
  9.7 158.6 %collective-permute-start = (f32[5,32,1]{2,1,0:T(8,128)S(1)}, f32[5,32,1]{2,1,0:T(8,128)S(1)}, u32[]{:S(2)}, u32[]{:S(2)}) collective-permute-start(f32[5,32,1]{2,1,0:T(8,128)S(1)} %get-tuple-element.8), channel_id=1, source_target_pairs={{0,8},{8,16},{16,24},{24,32},{32,40},{40,48},{48,56},{56,64},{64,7... | collective-permute-start | bytes 1928 | tf_op jit(solution)/shard_map/ppermute | solution.py:14
  29.3 38.4 %copy-start.5 = (f32[16,8192]{1,0:T(8,128)S(1)}, f32[16,8192]{1,0:T(8,128)}, u32[]{:S(2)}) copy-start(f32[16,8192]{1,0:T(8,128)} %param.16) | copy-start | bytes 1572868
  29.3 38.4 %copy-start.14 = (f32[16,5]{0,1:T(8,128)S(1)}, f32[16,5]{0,1:T(8,128)}, u32[]{:S(2)}) copy-start(f32[16,5]{0,1:T(8,128)} %param.20) | copy-start | bytes 964
  73.2 2.7 copy-start.13
  139.2 8.5 %copy-start.2 = (f32[5,32,2048]{2,1,0:T(8,128)S(1)}, f32[5,32,2048]{2,1,0:T(8,128)}, u32[]{:S(2)}) copy-start(f32[5,32,2048]{2,1,0:T(8,128)} %param.11) | copy-start | bytes 3932164
  139.2 147.6 %all-to-all-start = ((f32[16,32,512]{2,0,1:T(8,128)}), f32[16,32,512]{2,0,1:T(8,128)}, u32[]{:S(2)}, u32[]{:S(2)}) async-start(f32[16,32,512]{2,0,1:T(8,128)} %select_bitcast_fusion), calls=%async_computation | async-start | bytes 2097152 | tf_op jit(solution)/shard_map/all_to_all | solution.py:75
  147.7 12.3 %copy-start.15 = (f32[5,16]{1,0:T(8,128)S(1)}, f32[5,16]{1,0:T(8,128)}, u32[]{:S(2)}) copy-start(f32[5,16]{1,0:T(8,128)} %param.18) | copy-start | bytes 964
  168.3 6.8 %copy-start.17 = (f32[5,2]{0,1:T(2,128)S(1)}, f32[5,2]{0,1:T(2,128)}, u32[]{:S(2)}) copy-start(f32[5,2]{0,1:T(2,128)} %param.15) | copy-start | bytes 124
  168.3 1.0 copy-start.7
  168.3 1.0 copy-start.9
  169.3 63.3 %copy-start.4 = (f32[5,32,2050]{2,1,0:T(8,128)}, f32[5,32,2050]{2,1,0:T(8,128)S(1)}, u32[]{:S(2)}) copy-start(f32[5,32,2050]{2,1,0:T(8,128)S(1)} %concatenate.32) | copy-start | bytes 3936004
  169.4 83.7 %collective-permute-start.2 = (f32[5,1,2050]{2,1,0:T(1,128)S(1)}, f32[5,1,2050]{2,1,0:T(1,128)S(1)}, u32[]{:S(2)}, u32[]{:S(2)}) collective-permute-start(f32[5,1,2050]{2,1,0:T(1,128)S(1)} %get-tuple-element.5), channel_id=1, source_target_pairs={{1,0},{2,1},{3,2},{4,3},{5,4},{6,5},{7,6},{9,8},{10,9},{11,10},{12... | collective-permute-start | bytes 123008 | tf_op jit(solution)/shard_map/ppermute | solution.py:17
  173.0 80.1 %collective-permute-start.3 = (f32[5,1,2050]{2,1,0:T(1,128)S(1)}, f32[5,1,2050]{2,1,0:T(1,128)S(1)}, u32[]{:S(2)}, u32[]{:S(2)}) collective-permute-start(f32[5,1,2050]{2,1,0:T(1,128)S(1)} %get-tuple-element.4), channel_id=1, source_target_pairs={{0,1},{1,2},{2,3},{3,4},{4,5},{5,6},{6,7},{8,9},{9,10},{10,11},{11... | collective-permute-start | bytes 123008 | tf_op jit(solution)/shard_map/ppermute | solution.py:14
  232.6 20.5 %copy-start.6 = (f32[32,2048]{1,0:T(8,128)S(1)}, f32[32,2048]{1,0:T(8,128)}, u32[]{:S(2)}) copy-start(f32[32,2048]{1,0:T(8,128)} %param.12) | copy-start | bytes 786436
  232.6 20.5 %copy-start.8 = (f32[5,32,1]{2,1,0:T(8,128)S(1)}, f32[5,32,1]{2,1,0:T(8,128)}, u32[]{:S(2)}) copy-start(f32[5,32,1]{2,1,0:T(8,128)} %copy-done.7) | copy-start | bytes 1924
  232.6 20.5 %copy-start.10 = (f32[5,32,1]{2,1,0:T(8,128)S(1)}, f32[5,32,1]{2,1,0:T(8,128)}, u32[]{:S(2)}) copy-start(f32[5,32,1]{2,1,0:T(8,128)} %copy-done.9) | copy-start | bytes 1924
  232.6 20.5 %copy-start.16 = (f32[5]{0:T(128)S(1)}, f32[5]{0:T(128)}, u32[]{:S(2)}) copy-start(f32[5]{0:T(128)} %param.14) | copy-start | bytes 64
  257.2 7.5 %collective-permute-start.5 = (f32[5,32,1]{2,1,0:T(8,128)S(1)}, f32[5,32,1]{2,1,0:T(8,128)S(1)}, u32[]{:S(2)}, u32[]{:S(2)}) collective-permute-start(f32[5,32,1]{2,1,0:T(8,128)S(1)} %get-tuple-element.7), channel_id=1, source_target_pairs={{8,0},{16,8},{24,16},{32,24},{40,32},{48,40},{56,48},{64,56},{72,6... | collective-permute-start | bytes 1928 | tf_op jit(solution)/shard_map/ppermute | solution.py:17
  262.0 20.0 %copy-start.3 = (f32[5,32,2048]{2,1,0:T(8,128)S(1)}, f32[5,32,2048]{2,1,0:T(8,128)}, u32[]{:S(2)}) copy-start(f32[5,32,2048]{2,1,0:T(8,128)} %copy.34) | copy-start | bytes 3932164
  262.0 9.0 %collective-permute-start.4 = (f32[5,32,1]{2,1,0:T(8,128)S(1)}, f32[5,32,1]{2,1,0:T(8,128)S(1)}, u32[]{:S(2)}, u32[]{:S(2)}) collective-permute-start(f32[5,32,1]{2,1,0:T(8,128)S(1)} %get-tuple-element.6), channel_id=1, source_target_pairs={{0,8},{8,16},{16,24},{24,32},{32,40},{40,48},{48,56},{56,64},{64,7... | collective-permute-start | bytes 1928 | tf_op jit(solution)/shard_map/ppermute | solution.py:14
  271.1 1.5 copy-start.11
  273.8 4.8 %collective-permute-start.6 = (f32[5,1,2050]{2,1,0:T(1,128)S(1)}, f32[5,1,2050]{2,1,0:T(1,128)S(1)}, u32[]{:S(2)}, u32[]{:S(2)}) collective-permute-start(f32[5,1,2050]{2,1,0:T(1,128)S(1)} %get-tuple-element.3), channel_id=1, source_target_pairs={{1,0},{2,1},{3,2},{4,3},{5,4},{6,5},{7,6},{9,8},{10,9},{11,10},{12... | collective-permute-start | bytes 123008 | tf_op jit(solution)/shard_map/ppermute | solution.py:17
  276.7 5.3 %collective-permute-start.7 = (f32[5,1,2050]{2,1,0:T(1,128)S(1)}, f32[5,1,2050]{2,1,0:T(1,128)S(1)}, u32[]{:S(2)}, u32[]{:S(2)}) collective-permute-start(f32[5,1,2050]{2,1,0:T(1,128)S(1)} %get-tuple-element.2), channel_id=1, source_target_pairs={{0,1},{1,2},{2,3},{3,4},{4,5},{5,6},{6,7},{8,9},{9,10},{10,11},{11... | collective-permute-start | bytes 123008 | tf_op jit(solution)/shard_map/ppermute | solution.py:14
  282.0 7.1 %copy-start.1 = (f32[256,256]{1,0:T(8,128)S(1)}, f32[256,256]{1,0:T(8,128)}, u32[]{:S(2)}) copy-start(f32[256,256]{1,0:T(8,128)} %param.13) | copy-start | bytes 786436
where the time goes:
time: 291 us; the launch traced here: 289 us
  local copies, waits for them, and re-layouts  148 us (51%)
  other arithmetic  68.2 us (23%)
  starting transfers between devices  35.8 us (12%)
  matrix products  13.9 us (5%)
  blocking collectives  11.6 us (4%)
  waiting for transfers between devices  10.4 us (4%)
    gather x2, local copies, waits for them, and re-layouts, local(): outgoing = jnp.where(valid[None], moved[:, index], 0.0)  61.7 us
    scatter-add x1, other arithmetic, local(): deposit = jnp.zeros((nfield, rows * cols), jnp.float32).at[:, cell].add(p...  57.5 us
    gather x1, local copies, waits for them, and re-layouts, local(): local_fluid = fields.reshape(nfield, rows * cols)[:, cell]  38.3 us
    reshape x1, local copies, waits for them, and re-layouts, local(): deposit = jnp.zeros((nfield, rows * cols), jnp.float32).at[:, cell].add(p...  20.4 us
    ppermute x4, starting transfers between devices, padded_2(): lax.ppermute(lax.slice_in_dim(block, 0, width, axis=dim), axis, backward)  19.3 us
    unnamed x41, local copies, waits for them, and re-layouts  17.9 us
    all_gather x1, blocking collectives, local(): whole = lax.all_gather(profile, 'span', axis=1, tiled=True)  11.6 us
    ppermute x4, waiting for transfers between devices, padded_2(): lax.ppermute(lax.slice_in_dim(block, block.shape[dim] - width, None, axis...  9.78 us
  transfers between devices with their start and end apart: 9, of which 3 were waited for; matrix products, arithmetic and copies ran while one was open for 79% of the time, Pallas kernels for 0%

commit v1 on v0

v1 whole, which is shorter than its diff:
```python
import functools

import jax
import jax.numpy as jnp
from jax import lax
from jax.experimental import pallas as pl
from jax.experimental.pallas import tpu as pltpu
from jax.sharding import PartitionSpec as P

F32, BF = jnp.float32, jnp.bfloat16
MESH = pl.DeviceIdType.MESH
A, B, KB = 128, 512, 512


def step_kernel(
    n_pitch,
    n_span,
    cap,
    counts,
    cond_gain,
    advection,
    cell,
    fields,
    nu,
    mixing,
    parcels,
    couple,
    relax,
    drag,
    new_fields,
    arrived,
    offs,
    table,
    total,
    moved,
    records,
    outgoing,
    profile,
    source,
    state,
    row_out,
    row_in,
    col_out,
    col_in,
    send_sem,
    recv_sem,
    prof_send,
    prof_recv,
    halo_send,
    halo_recv,
    own_sem,
):
    nf, rows, cols = fields.shape
    nq, npar = parcels.shape
    chunks = cols // B
    blocks = npar // KB
    me, sp = lax.axis_index("pitch"), lax.axis_index("span")
    pitch_next, pitch_prev = lax.rem(me + 1, n_pitch), lax.rem(me + n_pitch - 1, n_pitch)
    span_next, span_prev = lax.rem(sp + 1, n_span), lax.rem(sp + n_span - 1, n_span)

    barrier = pltpu.get_barrier_semaphore()

    def greet_pitch(k, _):
        pl.semaphore_signal(
            barrier, inc=1, device_id=(lax.rem(me + k, n_pitch), sp), device_id_type=MESH
        )
        return 0

    def greet_span(k, _):
        pl.semaphore_signal(
            barrier, inc=1, device_id=(me, lax.rem(sp + k, n_span)), device_id_type=MESH
        )
        return 0

    lax.fori_loop(1, n_pitch, greet_pitch, 0)
    lax.fori_loop(1, n_span, greet_span, 0)

    running = jnp.int32(0)
    for p in range(n_pitch):
        offs[p] = running
        running = running + counts[p]
    first = offs[pitch_next] // KB
    for s in range(blocks):
        records[s] = parcels[:, s * KB : (s + 1) * KB]

    for f in range(nf):
        for q in range(chunks):
            x = fields[f, :, q * B : (q + 1) * B]
            hi = x.astype(BF)
            at = f * A + q * rows
            table[at : at + rows, 0:B] = hi
            table[at : at + rows, B : 2 * B] = (x - hi.astype(F32)).astype(BF)

    lane = lax.broadcasted_iota(jnp.int32, (rows, 128), 1)
    mean = jnp.zeros((rows, 128), F32)
    left = jnp.zeros((rows, 128), F32)
    right = jnp.zeros((rows, 128), F32)
    for f in range(nf):
        x = fields[f]
        mean = jnp.where(lane == f, jnp.sum(x, axis=1, keepdims=True) * (1.0 / cols), mean)
        left = jnp.where(lane == f, x[:, 0:1], left)
        right = jnp.where(lane == f, x[:, cols - 1 : cols], right)
        row_out[0, f : f + 1, :] = x[0:1, :]
        row_out[1, f : f + 1, :] = x[rows - 1 : rows, :]
    col_out[0] = left
    col_out[1] = right
    mine = pl.ds(pl.multiple_of(sp * rows, rows), rows)
    profile[mine, :] = mean

    diag = lax.broadcasted_iota(jnp.int32, (nq, nq), 0) == lax.broadcasted_iota(
        jnp.int32, (nq, nq), 1
    )

    def column(line):
        return jnp.sum(jnp.where(diag, line, 0.0), axis=1, keepdims=True)

    keep = column(1.0 - relax[...])
    pull = [column(drag[f : f + 1, :]) for f in range(nf)]
    cp = couple[...]
    index_a = lax.broadcasted_iota(jnp.int32, (A, KB), 0)
    index_b = lax.broadcasted_iota(jnp.int32, (B, KB), 0)
    lane_q = lax.broadcasted_iota(jnp.int32, (nq, 128), 1)

    def block_of(s):
        return lax.rem(first + s, blocks)

    def cells_of(block):
        homes = cell[block]
        c = jnp.concatenate([homes[q : q + 1] for q in range(KB // 128)], axis=1)
        in_row = c & (cols - 1)
        hot_a = index_a == (in_row // B) * rows + c // cols
        hot_b = jnp.where(index_b == (in_row & (B - 1)), 1.0, 0.0).astype(BF)
        return hot_a, hot_b

    def gather(s):
        block = block_of(s)
        hot_a, hot_b = cells_of(block)
        picked = jnp.dot(
            table[...], jnp.concatenate([hot_b, hot_b], axis=0), preferred_element_type=F32
        )
        value = keep * records[block]
        for f in range(nf):
            fluid = jnp.sum(
                jnp.where(hot_a, picked[f * A : (f + 1) * A], 0.0), axis=0, keepdims=True
            )
            value = value + pull[f] * fluid
        for q in range(KB // 128):
            moved[s * (KB // 128) + q] = value[:, q * 128 : (q + 1) * 128]

    def pack(k, slot):
        p = lax.rem(me + k, n_pitch)
        count = counts[p]
        start = lax.rem(offs[p] - first * KB + npar, npar)
        tile = start // 128
        pieces = [moved[tile + q] for q in range(cap // 128 + 1)]
        shift = jnp.full((nq, 128), lax.rem(start, 128), jnp.int32)
        for bit in range(7):
            by = 1 << bit
            turned = [pltpu.roll(piece, 128 - by, axis=1) for piece in pieces]
            turned.append(turned[-1])
            pieces = [
                jnp.where(
                    (shift & by) != 0,
                    jnp.where(lane_q < 128 - by, turned[q], turned[q + 1]),
                    pieces[q],
                )
                for q in range(len(pieces))
            ]
        for q in range(cap // 128):
            outgoing[slot, :, q * 128 : (q + 1) * 128] = jnp.where(
                lane_q + q * 128 < count, pieces[q], 0.0
            )

    own_slots = pl.ds(pl.multiple_of(me * cap, cap), cap)

    def parcel_copy(k):
        return pltpu.make_async_remote_copy(
            src_ref=outgoing.at[k],
            dst_ref=arrived.at[:, own_slots],
            send_sem=send_sem.at[k],
            recv_sem=recv_sem.at[k],
            device_id=(lax.rem(me + k, n_pitch), sp),
            device_id_type=MESH,
        )

    def profile_copy(k):
        return pltpu.make_async_remote_copy(
            src_ref=profile.at[mine],
            dst_ref=profile.at[mine],
            send_sem=prof_send.at[k],
            recv_sem=prof_recv.at[k],
            device_id=(me, lax.rem(sp + k, n_span)),
            device_id_type=MESH,
        )

    def halo_copies(turn):
        copies = []
        for side in range(2):
            for kind, (out, into, target) in enumerate(
                (
                    (row_out, row_in, (me, (span_prev, span_next)[side])),
                    (col_out, col_in, ((pitch_prev, pitch_next)[side], sp)),
                )
            ):
                copies.append(
                    pltpu.make_async_remote_copy(
                        src_ref=out.at[2 * turn + side],
                        dst_ref=into.at[2 * turn + side],
                        send_sem=halo_send.at[4 * turn + 2 * side + kind],
                        recv_sem=halo_recv.at[4 * turn + 2 * side + kind],
                        device_id=target,
                        device_id_type=MESH,
                    )
                )
        return copies

    gather(0)
    for q in range(KB // 128):
        moved[npar // 128 + q] = moved[q]
    pl.semaphore_wait(barrier, n_pitch + n_span - 2)

    def start_profile(k, _):
        profile_copy(k).start()
        return 0

    lax.fori_loop(1, n_span, start_profile, 0)
    first_halo = halo_copies(0)
    for copy in first_halo:
        copy.start()

    def gather_and_send(s, _):
        gather(s)
        pack(s, s)
        parcel_copy(s).start()
        return 0

    lax.fori_loop(1, blocks, gather_and_send, 0)

    def send(k, _):
        pack(k, k)
        parcel_copy(k).start()
        return 0

    lax.fori_loop(blocks, n_pitch, send, 0)
    pack(n_pitch, 0)
    own_copy = pltpu.make_async_copy(outgoing.at[0], arrived.at[:, own_slots], own_sem)
    own_copy.start()

    total[...] = jnp.zeros_like(total)

    def scatter(s, _):
        hot_a, hot_b = cells_of(s)
        par = records[s]
        given = jnp.zeros((nf, KB), F32)
        for q in range(nq):
            given = given + cp[:, q : q + 1] * par[q : q + 1, :]
        hi = given.astype(BF).astype(F32)
        lo = given - hi
        spread = jnp.concatenate(
            [
                jnp.concatenate(
                    [jnp.where(hot_a, x[f : f + 1], 0.0).astype(BF) for f in range(nf)], axis=0
                )
                for x in (hi, lo)
            ],
            axis=1,
        )
        total[...] += lax.dot_general(
            spread,
            jnp.concatenate([hot_b, hot_b], axis=1),
            (((1,), (1,)), ((), ())),
            preferred_element_type=F32,
        )
        return 0

    lax.fori_loop(0, blocks, scatter, 0)

    def wait_profile(k, _):
        profile_copy(k).wait()
        return 0

    lax.fori_loop(1, n_span, wait_profile, 0)
    corr = jnp.dot(
        mixing[mine, :], profile[...], precision=lax.Precision.HIGHEST, preferred_element_type=F32
    )
    x = fields[0] + corr[:, 0:1]
    rate = (jnp.maximum(x, 0.0) + jnp.log1p(jnp.exp(-jnp.abs(x)))) * (
        1.0 + jnp.tanh(fields[1] + corr[:, 1:2])
    )
    source[0] = rate
    for f in reversed(range(nf)):
        deposit = jnp.concatenate(
            [total[f * A + q * rows : f * A + (q + 1) * rows, :] for q in range(chunks)], axis=1
        )
        source[f] = 0.25 * (cond_gain[f] * rate - 0.5 * corr[:, f : f + 1] + deposit)

    row_id = lax.broadcasted_iota(jnp.int32, (rows, cols), 0)
    col_id = lax.broadcasted_iota(jnp.int32, (rows, cols), 1)
    row_low = jnp.where(sp == 0, 0.0, 1.0)
    row_high = jnp.where(sp == n_span - 1, 0.0, 1.0)
    col_low = jnp.where(me == 0, 0.0, 1.0)
    col_high = jnp.where(me == n_pitch - 1, 0.0, 1.0)

    def advance(u, f, turn):
        below = row_in[2 * turn + 1, f : f + 1, :] * row_low
        above = row_in[2 * turn, f : f + 1, :] * row_high
        before = col_in[2 * turn + 1][:, f : f + 1] * col_low
        after = col_in[2 * turn][:, f : f + 1] * col_high
        upper = jnp.where(row_id == rows - 1, above, pltpu.roll(u, rows - 1, axis=0))
        lower = jnp.where(row_id == 0, below, pltpu.roll(u, 1, axis=0))
        ahead = jnp.where(col_id == cols - 1, after, pltpu.roll(u, cols - 1, axis=1))
        behind = jnp.where(col_id == 0, before, pltpu.roll(u, 1, axis=1))
        return (
            u
            + source[f]
            + advection[0, f] * (upper - lower)
            + advection[1, f] * (ahead - behind)
            + nu[...] * (upper + lower + ahead + behind - 4.0 * u)
        )

    for copy in first_halo:
        copy.wait()
    left = jnp.zeros((rows, 128), F32)
    right = jnp.zeros((rows, 128), F32)
    for f in range(nf):
        u = advance(fields[f], f, 0)
        state[f] = u
        left = jnp.where(lane == f, u[:, 0:1], left)
        right = jnp.where(lane == f, u[:, cols - 1 : cols], right)
        row_out[2, f : f + 1, :] = u[0:1, :]
        row_out[3, f : f + 1, :] = u[rows - 1 : rows, :]
    col_out[2] = left
    col_out[3] = right
    second_halo = halo_copies(1)
    for copy in second_halo:
        copy.start()
    for copy in second_halo:
        copy.wait()
    for f in range(nf):
        new_fields[f] = advance(state[f], f, 1)

    own_copy.wait()

    def wait_parcels(k, _):
        parcel_copy(k).wait()
        return 0

    lax.fori_loop(1, n_pitch, wait_parcels, 0)


def local(
    fields, diffusivity, mixing, cond_gain, advection, parcels, cell, couple, relax, drag, counts
):
    nf, rows, cols = fields.shape
    nq, npar = parcels.shape
    n_pitch, n_span = lax.axis_size("pitch"), lax.axis_size("span")
    cap = 2 * npar // n_pitch
    vmem = pl.BlockSpec(memory_space=pltpu.VMEM)
    smem = pl.BlockSpec(memory_space=pltpu.SMEM)
    dma = pltpu.SemaphoreType.DMA
    return pl.pallas_call(
        functools.partial(step_kernel, n_pitch, n_span, cap),
        out_shape=(
            jax.ShapeDtypeStruct(fields.shape, F32),
            jax.ShapeDtypeStruct((nq, n_pitch * cap), F32),
        ),
        in_specs=[smem] * 3 + [vmem] * 8,
        out_specs=(vmem, pl.BlockSpec(memory_space=pl.ANY)),
        scratch_shapes=[
            pltpu.SMEM((n_pitch,), jnp.int32),
            pltpu.VMEM((nf * A, 2 * B), BF),
            pltpu.VMEM((nf * A, B), F32),
            pltpu.VMEM(((npar + KB) // 128, nq, 128), F32),
            pltpu.VMEM((npar // KB, nq, KB), F32),
            pltpu.VMEM((n_pitch, nq, cap), F32),
            pltpu.VMEM((n_span * rows, 128), F32),
            pltpu.VMEM(fields.shape, F32),
            pltpu.VMEM(fields.shape, F32),
            pltpu.VMEM((4, 8, cols), F32),
            pltpu.VMEM((4, 8, cols), F32),
            pltpu.VMEM((4, rows, 128), F32),
            pltpu.VMEM((4, rows, 128), F32),
            dma((n_pitch,)),
            dma((n_pitch,)),
            dma((n_span,)),
            dma((n_span,)),
            dma((8,)),
            dma((8,)),
            dma,
        ],
        compiler_params=pltpu.CompilerParams(
            collective_id=0, has_side_effects=True, vmem_limit_bytes=48 << 20
        ),
        cost_estimate=pl.CostEstimate(
            flops=8 * nf * rows * cols * npar, bytes_accessed=6 << 20, transcendentals=0
        ),
    )(
        counts,
        cond_gain,
        advection.T,
        cell.reshape(npar // KB, KB // 128, 128),
        fields,
        diffusivity,
        mixing,
        parcels,
        couple,
        relax.reshape(1, nq),
        drag.T,
    )


def solution(mesh):
    return jax.shard_map(
        local,
        mesh=mesh,
        in_specs=(
            P(None, "span", "pitch"),
            P("span", "pitch"),
            P(),
            P(),
            P(),
            P(None, ("pitch", "span")),
            P(("pitch", "span")),
            P(),
            P(),
            P(),
            P(("pitch", "span")),
        ),
        out_specs=(P(None, "span", "pitch"), P(None, ("pitch", "span"))),
        check_vma=False,
    )
```

time: 291 us -> 77.4 us (0.27)
  the two profiles are of different devices: /device:TPU:28 before, /device:TPU:1 now
where the time goes in v1:
time: 77.4 us; the launch traced here: 77 us
  Pallas kernels  65.3 us (84%)
  local copies, waits for them, and re-layouts  11.1 us (14%)
    pallas_call x1, Pallas kernels, local(): pl.pallas_call(functools.partial(step_kernel, n_pitch, n_span, cap), out_...  65.3 us
    unnamed x24, local copies, waits for them, and re-layouts  11.1 us

profile of v1, /device:TPU:1, one launch (start us, length us, event | category | flops | bytes accessed | tf_op | source)
XLA Modules:
  0.0 77.0 jit_solution(319248913914035475)
XLA Ops:
  0.6 0.0 copy-start
  0.6 1.3 %copy-done = f32[5,32,2048]{2,1,0:T(8,128)S(1)} copy-done((f32[5,32,2048]{2,1,0:T(8,128)S(1)}, f32[5,32,2048]{2,1,0:T(8,128)}, u32[]{:S(2)}) %copy-start) | copy-done | bytes 1310744
  2.0 0.0 copy-start.1
  2.0 1.0 %copy-done.1 = f32[16,8192]{1,0:T(8,128)S(1)} copy-done((f32[16,8192]{1,0:T(8,128)S(1)}, f32[16,8192]{1,0:T(8,128)}, u32[]{:S(2)}) %copy-start.1) | copy-done | bytes 524312
  3.0 0.0 copy-start.2
  3.0 0.9 %copy-done.2 = f32[32,2048]{1,0:T(8,128)S(1)} copy-done((f32[32,2048]{1,0:T(8,128)S(1)}, f32[32,2048]{1,0:T(8,128)}, u32[]{:S(2)}) %copy-start.2) | copy-done | bytes 262168
  3.9 0.0 copy-start.3
  3.9 0.9 %copy-done.3 = f32[256,256]{1,0:T(8,128)S(1)} copy-done((f32[256,256]{1,0:T(8,128)S(1)}, f32[256,256]{1,0:T(8,128)}, u32[]{:S(2)}) %copy-start.3) | copy-done | bytes 262168
  4.9 0.0 copy-start.4
  4.9 0.8 copy-done.4
  5.7 0.0 copy-start.5
  5.7 0.7 copy-done.5
  6.3 0.0 copy-start.6
  6.3 0.7 copy-done.6
  7.0 0.0 copy-start.7
  7.0 0.7 copy-done.7
  7.7 0.0 copy-start.8
  7.7 0.7 copy-done.8
  8.4 0.0 copy-start.9
  8.4 0.7 copy-done.9
  9.0 0.0 copy-start.10
  9.0 0.7 copy-done.10
  9.7 65.3 %shard_map.122 = (f32[5,32,2048]{2,1,0:T(8,128)S(1)}, f32[16,16384]{1,0:T(8,128)S(1)}) custom-call(s32[32]{0:T(128)S(1)} %copy-done.8, f32[5]{0:T(128)S(1)} %copy-done.9, f32[2,5]{1,0:T(2,128)S(1)} %bitcast.6, s32[16,4,128]{2,1,0:T(4,128)S(1)} %bitcast.4, f32[5,32,2048]{2,1,0:T(8,128)S(1)} %copy-done, f32[32,2048]{1,0:T(8,128)S(1)} %copy-done.2, ...), custom_call_target="tpu_custom_call" | custom-call | flops 21474836480 | bytes 6291456 | tf_op jit(solution)/shard_map/pallas_call | solution.py:361
  75.0 1.1 %copy.15 = f32[5,32,2048]{2,1,0:T(8,128)} copy(f32[5,32,2048]{2,1,0:T(8,128)S(1)} %get-tuple-element.4) | data formatting | bytes 2621440
  76.1 1.0 %copy.16 = f32[16,16384]{1,0:T(8,128)} copy(f32[16,16384]{1,0:T(8,128)S(1)} %get-tuple-element.5) | data formatting | bytes 2097152
Async XLA Ops:
  0.6 1.3 %copy-start = (f32[5,32,2048]{2,1,0:T(8,128)S(1)}, f32[5,32,2048]{2,1,0:T(8,128)}, u32[]{:S(2)}) copy-start(f32[5,32,2048]{2,1,0:T(8,128)} %fields.1) | copy-start | bytes 3932164
  2.0 1.0 %copy-start.1 = (f32[16,8192]{1,0:T(8,128)S(1)}, f32[16,8192]{1,0:T(8,128)}, u32[]{:S(2)}) copy-start(f32[16,8192]{1,0:T(8,128)} %parcels.1) | copy-start | bytes 1572868
  3.0 0.9 %copy-start.2 = (f32[32,2048]{1,0:T(8,128)S(1)}, f32[32,2048]{1,0:T(8,128)}, u32[]{:S(2)}) copy-start(f32[32,2048]{1,0:T(8,128)} %nu.1) | copy-start | bytes 786436
  3.9 0.9 %copy-start.3 = (f32[256,256]{1,0:T(8,128)S(1)}, f32[256,256]{1,0:T(8,128)}, u32[]{:S(2)}) copy-start(f32[256,256]{1,0:T(8,128)} %mixing.1) | copy-start | bytes 786436
  4.9 0.8 copy-start.4
  5.7 0.7 copy-start.5
  6.3 0.7 copy-start.6
  7.0 0.7 copy-start.7
  7.7 0.7 copy-start.8
  8.4 0.7 copy-start.9
  9.0 0.7 copy-start.10

commit v2 on v1

--- a/solution.py
+++ b/solution.py
@@ -16,6 +16,19 @@
     n_pitch,
     n_span,
     cap,
+    counts_hbm,
+    gain_hbm,
+    advection_hbm,
+    cell_hbm,
+    fields_hbm,
+    nu_hbm,
+    mixing_hbm,
+    parcels_hbm,
+    couple_hbm,
+    relax_hbm,
+    drag_hbm,
+    new_fields,
+    arrived,
     counts,
     cond_gain,
     advection,
@@ -23,12 +36,11 @@
     fields,
     nu,
     mixing,
-    parcels,
     couple,
     relax,
     drag,
-    new_fields,
-    arrived,
+    load_sem,
+    record_sem,
     offs,
     table,
     total,
@@ -51,13 +63,42 @@
     own_sem,
 ):
     nf, rows, cols = fields.shape
-    nq, npar = parcels.shape
+    nq, npar = parcels_hbm.shape
     chunks = cols // B
     blocks = npar // KB
     me, sp = lax.axis_index("pitch"), lax.axis_index("span")
     pitch_next, pitch_prev = lax.rem(me + 1, n_pitch), lax.rem(me + n_pitch - 1, n_pitch)
     span_next, span_prev = lax.rem(sp + 1, n_span), lax.rem(sp + n_span - 1, n_span)
 
+    loads = {}
+    for n, (name, there, here) in enumerate(
+        (
+            ("counts", counts_hbm, counts),
+            ("fields", fields_hbm, fields),
+            ("cell", cell_hbm, cell),
+            ("relax", relax_hbm, relax),
+            ("drag", drag_hbm, drag),
+            ("couple", couple_hbm, couple),
+            ("mixing", mixing_hbm, mixing),
+            ("nu", nu_hbm, nu),
+            ("gain", gain_hbm, cond_gain),
+            ("advection", advection_hbm, advection),
+        )
+    ):
+        loads[name] = pltpu.make_async_copy(there, here, load_sem.at[n])
+    for name in ("counts", "fields", "cell", "relax", "drag"):
+        loads[name].start()
+    record_loads = [
+        pltpu.make_async_copy(
+            parcels_hbm.at[:, s * KB : (s + 1) * KB], records.at[s], record_sem.at[s]
+        )
+        for s in range(blocks)
+    ]
+    for load in record_loads:
+        load.start()
+    for name in ("couple", "mixing", "nu", "gain", "advection"):
+        loads[name].start()
+
     barrier = pltpu.get_barrier_semaphore()
 
     def greet_pitch(k, _):
@@ -75,13 +116,13 @@
     lax.fori_loop(1, n_pitch, greet_pitch, 0)
     lax.fori_loop(1, n_span, greet_span, 0)
 
+    loads["counts"].wait()
     running = jnp.int32(0)
     for p in range(n_pitch):
         offs[p] = running
         running = running + counts[p]
     first = offs[pitch_next] // KB
-    for s in range(blocks):
-        records[s] = parcels[:, s * KB : (s + 1) * KB]
+    loads["fields"].wait()
 
     for f in range(nf):
         for q in range(chunks):
@@ -114,6 +155,8 @@
     def column(line):
         return jnp.sum(jnp.where(diag, line, 0.0), axis=1, keepdims=True)
 
+    for name in ("cell", "relax", "drag", "couple"):
+        loads[name].wait()
     keep = column(1.0 - relax[...])
     pull = [column(drag[f : f + 1, :]) for f in range(nf)]
     cp = couple[...]
@@ -153,22 +196,12 @@
         start = lax.rem(offs[p] - first * KB + npar, npar)
         tile = start // 128
         pieces = [moved[tile + q] for q in range(cap // 128 + 1)]
-        shift = jnp.full((nq, 128), lax.rem(start, 128), jnp.int32)
-        for bit in range(7):
-            by = 1 << bit
-            turned = [pltpu.roll(piece, 128 - by, axis=1) for piece in pieces]
-            turned.append(turned[-1])
-            pieces = [
-                jnp.where(
-                    (shift & by) != 0,
-                    jnp.where(lane_q < 128 - by, turned[q], turned[q + 1]),
-                    pieces[q],
-                )
-                for q in range(len(pieces))
-            ]
+        shift = lax.rem(start, 128)
+        turned = [pltpu.roll(piece, lax.rem(128 - shift, 128), axis=1) for piece in pieces]
         for q in range(cap // 128):
+            piece = jnp.where(lane_q < 128 - shift, turned[q], turned[q + 1])
             outgoing[slot, :, q * 128 : (q + 1) * 128] = jnp.where(
-                lane_q + q * 128 < count, pieces[q], 0.0
+                lane_q + q * 128 < count, piece, 0.0
             )
 
     own_slots = pl.ds(pl.multiple_of(me * cap, cap), cap)
@@ -214,6 +247,8 @@
                 )
         return copies
 
+    for load in record_loads:
+        load.wait()
     gather(0)
     for q in range(KB // 128):
         moved[npar // 128 + q] = moved[q]
@@ -280,6 +315,8 @@
         return 0
 
     lax.fori_loop(1, n_span, wait_profile, 0)
+    for name in ("mixing", "nu", "gain", "advection"):
+        loads[name].wait()
     corr = jnp.dot(
         mixing[mine, :], profile[...], precision=lax.Precision.HIGHEST, preferred_element_type=F32
     )
@@ -356,7 +393,7 @@
     n_pitch, n_span = lax.axis_size("pitch"), lax.axis_size("span")
     cap = 2 * npar // n_pitch
     vmem = pl.BlockSpec(memory_space=pltpu.VMEM)
-    smem = pl.BlockSpec(memory_space=pltpu.SMEM)
+    hbm = pl.BlockSpec(memory_space=pl.ANY)
     dma = pltpu.SemaphoreType.DMA
     return pl.pallas_call(
         functools.partial(step_kernel, n_pitch, n_span, cap),
@@ -364,9 +401,21 @@
             jax.ShapeDtypeStruct(fields.shape, F32),
             jax.ShapeDtypeStruct((nq, n_pitch * cap), F32),
         ),
-        in_specs=[smem] * 3 + [vmem] * 8,
+        in_specs=[hbm] * 11,
         out_specs=(vmem, pl.BlockSpec(memory_space=pl.ANY)),
         scratch_shapes=[
+            pltpu.SMEM((n_pitch,), jnp.int32),
+            pltpu.SMEM((nf,), F32),
+            pltpu.SMEM((2, nf), F32),
+            pltpu.VMEM((npar // KB, KB // 128, 128), jnp.int32),
+            pltpu.VMEM(fields.shape, F32),
+            pltpu.VMEM((rows, cols), F32),
+            pltpu.VMEM(mixing.shape, F32),
+            pltpu.VMEM((nf, nq), F32),
+            pltpu.VMEM((1, nq), F32),
+            pltpu.VMEM((nf, nq), F32),
+            dma((10,)),
+            dma((npar // KB,)),
             pltpu.SMEM((n_pitch,), jnp.int32),
             pltpu.VMEM((nf * A, 2 * B), BF),
             pltpu.VMEM((nf * A, B), F32),
@@ -389,7 +438,7 @@
             dma,
         ],
         compiler_params=pltpu.CompilerParams(
-            collective_id=0, has_side_effects=True, vmem_limit_bytes=48 << 20
+            collective_id=0, has_side_effects=True, vmem_limit_bytes=60 << 20
         ),
         cost_estimate=pl.CostEstimate(
             flops=8 * nf * rows * cols * npar, bytes_accessed=6 << 20, transcendentals=0

time: 77.4 us -> 56.7 us (0.73)
  Pallas kernels: 65.3 us -> 52.3 us
  local copies, waits for them, and re-layouts: 11.1 us -> 3.56 us
    pallas_call x1, Pallas kernels: 65.3 us -> 52.3 us  [local(): pl.pallas_call(functools.partial(step_kernel, n_pitch, n_span, cap), out_...]
    unnamed x24 -> x4, local copies, waits for them, and re-layouts: 11.1 us -> 3.56 us
where the time goes in v2:
time: 56.7 us; the launch traced here: 56.6 us
  Pallas kernels  52.3 us (92%)
  local copies, waits for them, and re-layouts  3.56 us (6%)
  between operations  0.65 us (1%)
    pallas_call x1, Pallas kernels, local(): pl.pallas_call(functools.partial(step_kernel, n_pitch, n_span, cap), out_...  52.3 us
    unnamed x4, local copies, waits for them, and re-layouts  3.56 us

profile of v2, /device:TPU:1, one launch (start us, length us, event | category | flops | bytes accessed | tf_op | source)
XLA Modules:
  0.0 56.6 jit_solution(11257960314573573694)
XLA Ops:
  0.6 52.3 %shard_map.122 = (f32[5,32,2048]{2,1,0:T(8,128)}, f32[16,16384]{1,0:T(8,128)}) custom-call(s32[32]{0:T(128)} %counts_hbm.1, f32[5]{0:T(128)} %gain_hbm.1, f32[2,5]{1,0:T(2,128)} %bitcast.6, s32[16,4,128]{2,1,0:T(4,128)} %bitcast.4, f32[5,32,2048]{2,1,0:T(8,128)} %fields_hbm.1, f32[32,2048]{1,0:T(8,128)} %nu_hbm.1, f32[256,256]{1,0:T(8,128)} %mixing_hbm.1, ...), custom_call_target="tpu_custom_call" | custom-call | flops 21474836480 | bytes 6291456 | tf_op jit(solution)/shard_map/pallas_call | solution.py:398
  53.0 0.0 copy-start
  53.0 2.6 %copy.15 = f32[5,32,2048]{2,1,0:T(8,128)} copy(f32[5,32,2048]{2,1,0:T(8,128)} %get-tuple-element.4) | data formatting | bytes 2621440
  55.6 0.0 copy-done
  55.6 1.0 %copy.16 = f32[16,16384]{1,0:T(8,128)} copy(f32[16,16384]{1,0:T(8,128)S(1)} %copy-done) | data formatting | bytes 2097152
Async XLA Ops:
  53.0 2.6 %copy-start = (f32[16,16384]{1,0:T(8,128)S(1)}, f32[16,16384]{1,0:T(8,128)}, u32[]{:S(2)}) copy-start(f32[16,16384]{1,0:T(8,128)} %get-tuple-element.5) | copy-start | bytes 3145732

commit v3 on v2

--- a/solution.py
+++ b/solution.py
@@ -9,6 +9,7 @@
 
 F32, BF = jnp.float32, jnp.bfloat16
 MESH = pl.DeviceIdType.MESH
+AHEAD = 2
 A, B, KB = 128, 512, 512
 
 
@@ -43,6 +44,9 @@
     record_sem,
     offs,
     table,
+    place,
+    place_s,
+    place_sem,
     total,
     moved,
     records,
@@ -61,6 +65,7 @@
     halo_send,
     halo_recv,
     own_sem,
+    out_sem,
 ):
     nf, rows, cols = fields.shape
     nq, npar = parcels_hbm.shape
@@ -124,13 +129,21 @@
     first = offs[pitch_next] // KB
     loads["fields"].wait()
 
+    loads["cell"].wait()
+    lane_128 = lax.broadcasted_iota(jnp.int32, (KB // 128, 128), 1)
+    for s in range(blocks):
+        at = slice(s * (KB // 128), (s + 1) * (KB // 128))
+        place[0, at, :] = cell[s] // 128
+        place[1, at, :] = (lane_128 - cell[s]) & 127
+    place_copy = pltpu.make_async_copy(place, place_s, place_sem)
+    place_copy.start()
+
     for f in range(nf):
-        for q in range(chunks):
-            x = fields[f, :, q * B : (q + 1) * B]
-            hi = x.astype(BF)
-            at = f * A + q * rows
-            table[at : at + rows, 0:B] = hi
-            table[at : at + rows, B : 2 * B] = (x - hi.astype(F32)).astype(BF)
+        for r in range(0, rows, 8):
+            for q in range(cols // 128):
+                at = pl.ds((r * (cols // 128) + q) * 8 + f, 8, stride=cols // 16)
+                table[at, :] = fields[f, r : r + 8, q * 128 : (q + 1) * 128]
+    tiles = table.reshape(rows * cols // 128, 8, 128)
 
     lane = lax.broadcasted_iota(jnp.int32, (rows, 128), 1)
     mean = jnp.zeros((rows, 128), F32)
@@ -155,13 +168,14 @@
     def column(line):
         return jnp.sum(jnp.where(diag, line, 0.0), axis=1, keepdims=True)
 
-    for name in ("cell", "relax", "drag", "couple"):
+    for name in ("relax", "drag", "couple"):
         loads[name].wait()
     keep = column(1.0 - relax[...])
     pull = [column(drag[f : f + 1, :]) for f in range(nf)]
     cp = couple[...]
     index_a = lax.broadcasted_iota(jnp.int32, (A, KB), 0)
     index_b = lax.broadcasted_iota(jnp.int32, (B, KB), 0)
+    lane_8 = lax.broadcasted_iota(jnp.int32, (8, 128), 1)
     lane_q = lax.broadcasted_iota(jnp.int32, (nq, 128), 1)
 
     def block_of(s):
@@ -177,18 +191,16 @@
 
     def gather(s):
         block = block_of(s)
-        hot_a, hot_b = cells_of(block)
-        picked = jnp.dot(
-            table[...], jnp.concatenate([hot_b, hot_b], axis=0), preferred_element_type=F32
-        )
-        value = keep * records[block]
-        for f in range(nf):
-            fluid = jnp.sum(
-                jnp.where(hot_a, picked[f * A : (f + 1) * A], 0.0), axis=0, keepdims=True
-            )
-            value = value + pull[f] * fluid
-        for q in range(KB // 128):
-            moved[s * (KB // 128) + q] = value[:, q * 128 : (q + 1) * 128]
+        for h in range(KB // 128):
+            row = block * (KB // 128) + h
+            fluid = jnp.zeros((8, 128), F32)
+            for j in range(128):
+                found = pltpu.roll(tiles[place_s[0, row, j]], place_s[1, row, j], axis=1)
+                fluid = jnp.where(lane_8 == j, found, fluid)
+            value = keep * records[block, :, h * 128 : (h + 1) * 128]
+            for f in range(nf):
+                value = value + pull[f] * fluid[f : f + 1, :]
+            moved[s * (KB // 128) + h] = value
 
     def pack(k, slot):
         p = lax.rem(me + k, n_pitch)
@@ -249,9 +261,8 @@
 
     for load in record_loads:
         load.wait()
-    gather(0)
-    for q in range(KB // 128):
-        moved[npar // 128 + q] = moved[q]
+    place_copy.wait()
+    total[...] = jnp.zeros_like(total)
     pl.semaphore_wait(barrier, n_pitch + n_span - 2)
 
     def start_profile(k, _):
@@ -263,29 +274,10 @@
     for copy in first_halo:
         copy.start()
 
-    def gather_and_send(s, _):
-        gather(s)
-        pack(s, s)
-        parcel_copy(s).start()
-        return 0
-
-    lax.fori_loop(1, blocks, gather_and_send, 0)
-
-    def send(k, _):
-        pack(k, k)
-        parcel_copy(k).start()
-        return 0
-
-    lax.fori_loop(blocks, n_pitch, send, 0)
-    pack(n_pitch, 0)
-    own_copy = pltpu.make_async_copy(outgoing.at[0], arrived.at[:, own_slots], own_sem)
-    own_copy.start()
-
-    total[...] = jnp.zeros_like(total)
-
-    def scatter(s, _):
-        hot_a, hot_b = cells_of(s)
-        par = records[s]
+    def scatter(s):
+        block = block_of(s)
+        hot_a, hot_b = cells_of(block)
+        par = records[block]
         given = jnp.zeros((nf, KB), F32)
         for q in range(nq):
             given = given + cp[:, q : q + 1] * par[q : q + 1, :]
@@ -306,9 +298,28 @@
             (((1,), (1,)), ((), ())),
             preferred_element_type=F32,
         )
-        return 0
-
-    lax.fori_loop(0, blocks, scatter, 0)
+
+    def work(s, _):
+        gather(s)
+        scatter(s)
+        pack(s, s)
+
+        @pl.when(s >= 1)
+        def _():
+            parcel_copy(s).start()
+
+        return 0
+
+    lax.fori_loop(0, blocks, work, 0)
+    for q in range(KB // 128):
+        moved[npar // 128 + q] = moved[q]
+
+    def send(k, _):
+        pack(k, k)
+        parcel_copy(k).start()
+        return 0
+
+    lax.fori_loop(blocks, blocks + AHEAD, send, 0)
 
     def wait_profile(k, _):
         profile_copy(k).wait()
@@ -371,10 +382,18 @@
     second_halo = halo_copies(1)
     for copy in second_halo:
         copy.start()
+    lax.fori_loop(blocks + AHEAD, n_pitch, send, 0)
+    pack(n_pitch, 0)
+    own_copy = pltpu.make_async_copy(outgoing.at[0], arrived.at[:, own_slots], own_sem)
+    own_copy.start()
+
     for copy in second_halo:
         copy.wait()
     for f in range(nf):
-        new_fields[f] = advance(state[f], f, 1)
+        fields[f] = advance(state[f], f, 1)
+        pltpu.make_async_copy(fields.at[f], new_fields.at[f], out_sem.at[f]).start()
+    for f in range(nf):
+        pltpu.make_async_copy(fields.at[f], new_fields.at[f], out_sem.at[f]).wait()
 
     own_copy.wait()
 
@@ -383,6 +402,35 @@
         return 0
 
     lax.fori_loop(1, n_pitch, wait_parcels, 0)
+
+
+def hand_over_kernel(fields_from, arrived_from, fields_to, arrived_to, held, slots, sem_a, sem_b):
+    parts = sem_b.shape[1]
+    width = slots.shape[1] // parts
+    ways = [
+        (fields_from.at[f], held.at[f], fields_to.at[f], sem_a.at[0, f], sem_a.at[1, f])
+        for f in range(held.shape[0])
+    ]
+    for q in range(parts):
+        at = slice(q * width, (q + 1) * width)
+        ways.append(
+            (
+                arrived_from.at[:, at],
+                slots.at[:, at],
+                arrived_to.at[:, at],
+                sem_b.at[0, q],
+                sem_b.at[1, q],
+            )
+        )
+    into = [pltpu.make_async_copy(a, b, s) for a, b, _, s, _ in ways]
+    out = [pltpu.make_async_copy(b, c, s) for _, b, c, _, s in ways]
+    for copy in into:
+        copy.start()
+    for first, second in zip(into, out):
+        first.wait()
+        second.start()
+    for copy in out:
+        copy.wait()
 
 
 def local(
@@ -392,17 +440,16 @@
     nq, npar = parcels.shape
     n_pitch, n_span = lax.axis_size("pitch"), lax.axis_size("span")
     cap = 2 * npar // n_pitch
-    vmem = pl.BlockSpec(memory_space=pltpu.VMEM)
     hbm = pl.BlockSpec(memory_space=pl.ANY)
     dma = pltpu.SemaphoreType.DMA
-    return pl.pallas_call(
+    results = pl.pallas_call(
         functools.partial(step_kernel, n_pitch, n_span, cap),
         out_shape=(
             jax.ShapeDtypeStruct(fields.shape, F32),
             jax.ShapeDtypeStruct((nq, n_pitch * cap), F32),
         ),
         in_specs=[hbm] * 11,
-        out_specs=(vmem, pl.BlockSpec(memory_space=pl.ANY)),
+        out_specs=(hbm, hbm),
         scratch_shapes=[
             pltpu.SMEM((n_pitch,), jnp.int32),
             pltpu.SMEM((nf,), F32),
@@ -417,7 +464,10 @@
             dma((10,)),
             dma((npar // KB,)),
             pltpu.SMEM((n_pitch,), jnp.int32),
-            pltpu.VMEM((nf * A, 2 * B), BF),
+            pltpu.VMEM((rows * cols // 16, 128), F32),
+            pltpu.VMEM((2, npar // 128, 128), jnp.int32),
+            pltpu.SMEM((2, npar // 128, 128), jnp.int32),
+            dma,
             pltpu.VMEM((nf * A, B), F32),
             pltpu.VMEM(((npar + KB) // 128, nq, 128), F32),
             pltpu.VMEM((npar // KB, nq, KB), F32),
@@ -436,6 +486,7 @@
             dma((8,)),
             dma((8,)),
             dma,
+            dma((nf,)),
         ],
         compiler_params=pltpu.CompilerParams(
             collective_id=0, has_side_effects=True, vmem_limit_bytes=60 << 20
@@ -456,6 +507,19 @@
         relax.reshape(1, nq),
         drag.T,
     )
+    return pl.pallas_call(
+        hand_over_kernel,
+        out_shape=tuple(jax.ShapeDtypeStruct(x.shape, x.dtype) for x in results),
+        in_specs=[hbm] * 2,
+        out_specs=(hbm, hbm),
+        scratch_shapes=[
+            pltpu.VMEM(results[0].shape, F32),
+            pltpu.VMEM(results[1].shape, F32),
+            dma((2, nf)),
+            dma((2, 8)),
+        ],
+        compiler_params=pltpu.CompilerParams(vmem_limit_bytes=60 << 20),
+    )(*results)
 
 
 def solution(mesh):

time: 56.7 us -> 50.1 us (0.88)
  local copies, waits for them, and re-layouts: 3.56 us -> 0 us
  Pallas kernels: 52.3 us -> 49.3 us
    pallas_call x1, Pallas kernels: 52.3 us -> 46.4 us  [local(): pl.pallas_call(functools.partial(step_kernel, n_pitch, n_span, cap), out_...]
    unnamed x4 -> x0, local copies, waits for them, and re-layouts: 3.56 us -> none
    pallas_call x0 -> x1, Pallas kernels: none -> 2.89 us  [local(): pl.pallas_call(hand_over_kernel, out_shape=tuple((jax.ShapeDtypeStruct(x....]
where the time goes in v3:
time: 50.1 us; the launch traced here: 49.9 us
  Pallas kernels  49.3 us (98%)
  between operations  0.64 us (1%)
    pallas_call x1, Pallas kernels, local(): pl.pallas_call(functools.partial(step_kernel, n_pitch, n_span, cap), out_...  46.4 us
    pallas_call x1, Pallas kernels, local(): pl.pallas_call(hand_over_kernel, out_shape=tuple((jax.ShapeDtypeStruct(x....  2.89 us

profile of v3, /device:TPU:1, one launch (start us, length us, event | category | flops | bytes accessed | tf_op | source)
XLA Modules:
  0.0 49.9 jit_solution(5158727551532428419)
XLA Ops:
  0.6 46.4 %shard_map.122 = (f32[5,32,2048]{2,1,0:T(8,128)}, f32[16,16384]{1,0:T(8,128)}) custom-call(s32[32]{0:T(128)} %counts_hbm.1, f32[5]{0:T(128)} %gain_hbm.1, f32[2,5]{1,0:T(2,128)} %bitcast.6, s32[16,4,128]{2,1,0:T(4,128)} %bitcast.4, f32[5,32,2048]{2,1,0:T(8,128)} %fields_hbm.1, f32[32,2048]{1,0:T(8,128)} %nu_hbm.1, f32[256,256]{1,0:T(8,128)} %mixing_hbm.1, ...), custom_call_target="tpu_custom_call" | custom-call | flops 21474836480 | bytes 6291456 | tf_op jit(solution)/shard_map/pallas_call | solution.py:445
  47.0 2.9 %shard_map.123 = (f32[5,32,2048]{2,1,0:T(8,128)}, f32[16,16384]{1,0:T(8,128)}) custom-call(f32[5,32,2048]{2,1,0:T(8,128)} %get-tuple-element.4.fields_from, f32[16,16384]{1,0:T(8,128)} %get-tuple-element.5.arrived_from), custom_call_target="tpu_custom_call" | custom-call | tf_op jit(solution)/shard_map/pallas_call | solution.py:510

commit v4 on v3

--- a/solution.py
+++ b/solution.py
@@ -9,7 +9,9 @@
 
 F32, BF = jnp.float32, jnp.bfloat16
 MESH = pl.DeviceIdType.MESH
+ALONE = 12
 AHEAD = 2
+EACH = 2
 A, B, KB = 128, 512, 512
 
 
@@ -44,6 +46,9 @@
     record_sem,
     offs,
     table,
+    pair,
+    corr,
+    rate,
     place,
     place_s,
     place_sem,
@@ -91,7 +96,7 @@
         )
     ):
         loads[name] = pltpu.make_async_copy(there, here, load_sem.at[n])
-    for name in ("counts", "fields", "cell", "relax", "drag"):
+    for name in ("cell", "counts", "fields", "relax", "drag"):
         loads[name].start()
     record_loads = [
         pltpu.make_async_copy(
@@ -120,14 +125,6 @@
 
     lax.fori_loop(1, n_pitch, greet_pitch, 0)
     lax.fori_loop(1, n_span, greet_span, 0)
-
-    loads["counts"].wait()
-    running = jnp.int32(0)
-    for p in range(n_pitch):
-        offs[p] = running
-        running = running + counts[p]
-    first = offs[pitch_next] // KB
-    loads["fields"].wait()
 
     loads["cell"].wait()
     lane_128 = lax.broadcasted_iota(jnp.int32, (KB // 128, 128), 1)
@@ -138,11 +135,26 @@
     place_copy = pltpu.make_async_copy(place, place_s, place_sem)
     place_copy.start()
 
+    loads["counts"].wait()
+    running = jnp.int32(0)
+    for p in range(n_pitch):
+        offs[p] = running
+        running = running + counts[p]
+    first = offs[pitch_next] // KB
+    loads["fields"].wait()
+
     for f in range(nf):
         for r in range(0, rows, 8):
             for q in range(cols // 128):
                 at = pl.ds((r * (cols // 128) + q) * 8 + f, 8, stride=cols // 16)
                 table[at, :] = fields[f, r : r + 8, q * 128 : (q + 1) * 128]
+    for f in range(nf):
+        for q in range(chunks):
+            x = fields[f, :, q * B : (q + 1) * B]
+            hi = x.astype(BF)
+            at = f * A + q * rows
+            pair[at : at + rows, 0:B] = hi
+            pair[at : at + rows, B : 2 * B] = (x - hi.astype(F32)).astype(BF)
     tiles = table.reshape(rows * cols // 128, 8, 128)
 
     lane = lax.broadcasted_iota(jnp.int32, (rows, 128), 1)
@@ -181,17 +193,32 @@
     def block_of(s):
         return lax.rem(first + s, blocks)
 
-    def cells_of(block):
+    def cells_of(block, low):
         homes = cell[block]
-        c = jnp.concatenate([homes[q : q + 1] for q in range(KB // 128)], axis=1)
+        c = jnp.concatenate([homes[q : q + 1] for q in range(low, KB // 128)], axis=1)
         in_row = c & (cols - 1)
-        hot_a = index_a == (in_row // B) * rows + c // cols
-        hot_b = jnp.where(index_b == (in_row & (B - 1)), 1.0, 0.0).astype(BF)
+        hot_a = index_a[:, low * 128 :] == (in_row // B) * rows + c // cols
+        hot_b = jnp.where(index_b[:, low * 128 :] == (in_row & (B - 1)), 1.0, 0.0).astype(BF)
         return hot_a, hot_b
 
-    def gather(s):
+    def gather_by_matmul(s, low):
         block = block_of(s)
-        for h in range(KB // 128):
+        hot_a, hot_b = cells_of(block, low)
+        picked = jnp.dot(
+            pair[...], jnp.concatenate([hot_b, hot_b], axis=0), preferred_element_type=F32
+        )
+        value = keep * records[block, :, low * 128 :]
+        for f in range(nf):
+            fluid = jnp.sum(
+                jnp.where(hot_a, picked[f * A : (f + 1) * A], 0.0), axis=0, keepdims=True
+            )
+            value = value + pull[f] * fluid
+        for q in range(low, KB // 128):
+            moved[s * (KB // 128) + q] = value[:, (q - low) * 128 : (q - low + 1) * 128]
+
+    def gather(s, high):
+        block = block_of(s)
+        for h in range(high):
             row = block * (KB // 128) + h
             fluid = jnp.zeros((8, 128), F32)
             for j in range(128):
@@ -263,46 +290,61 @@
         load.wait()
     place_copy.wait()
     total[...] = jnp.zeros_like(total)
-    pl.semaphore_wait(barrier, n_pitch + n_span - 2)
 
     def start_profile(k, _):
         profile_copy(k).start()
         return 0
 
-    lax.fori_loop(1, n_span, start_profile, 0)
     first_halo = halo_copies(0)
-    for copy in first_halo:
-        copy.start()
-
-    def scatter(s):
-        block = block_of(s)
-        hot_a, hot_b = cells_of(block)
-        par = records[block]
-        given = jnp.zeros((nf, KB), F32)
-        for q in range(nq):
-            given = given + cp[:, q : q + 1] * par[q : q + 1, :]
-        hi = given.astype(BF).astype(F32)
-        lo = given - hi
-        spread = jnp.concatenate(
-            [
-                jnp.concatenate(
-                    [jnp.where(hot_a, x[f : f + 1], 0.0).astype(BF) for f in range(nf)], axis=0
+
+    def scatter(steps):
+        left_side, right_side = [], []
+        for s in steps:
+            block = block_of(s)
+            hot_a, hot_b = cells_of(block, 0)
+            par = records[block]
+            given = jnp.zeros((nf, KB), F32)
+            for q in range(nq):
+                given = given + cp[:, q : q + 1] * par[q : q + 1, :]
+            hi = given.astype(BF).astype(F32)
+            lo = given - hi
+            for x in (hi, lo):
+                left_side.append(
+                    jnp.concatenate(
+                        [jnp.where(hot_a, x[f : f + 1], 0.0).astype(BF) for f in range(nf)],
+                        axis=0,
+                    )
                 )
-                for x in (hi, lo)
-            ],
-            axis=1,
-        )
+                right_side.append(hot_b)
         total[...] += lax.dot_general(
-            spread,
-            jnp.concatenate([hot_b, hot_b], axis=1),
+            jnp.concatenate(left_side, axis=1),
+            jnp.concatenate(right_side, axis=1),
             (((1,), (1,)), ((), ())),
             preferred_element_type=F32,
         )
 
-    def work(s, _):
-        gather(s)
-        scatter(s)
+    def wait_profile(k, _):
+        profile_copy(k).wait()
+        return 0
+
+    def rate_of(part, parts):
+        at = pl.ds(pl.multiple_of(part * (cols // parts), cols // parts), cols // parts)
+        x = fields[0, :, at] + corr[:, 0:1]
+        rate[:, at] = (jnp.maximum(x, 0.0) + jnp.log1p(jnp.exp(-jnp.abs(x)))) * (
+            1.0 + jnp.tanh(fields[1, :, at] + corr[:, 1:2])
+        )
+
+    def gather_only(s, _):
+        gather(s, KB // 256)
+        gather_by_matmul(s, KB // 256)
         pack(s, s)
+
+        @pl.when(s == 0)
+        def _():
+            pl.semaphore_wait(barrier, n_pitch + n_span - 2)
+            lax.fori_loop(1, n_span, start_profile, 0)
+            for copy in first_halo:
+                copy.start()
 
         @pl.when(s >= 1)
         def _():
@@ -310,7 +352,23 @@
 
         return 0
 
-    lax.fori_loop(0, blocks, work, 0)
+    lax.fori_loop(0, ALONE, gather_only, 0)
+    for name in ("mixing", "nu", "gain", "advection"):
+        loads[name].wait()
+    lax.fori_loop(1, n_span, wait_profile, 0)
+    corr[...] = jnp.dot(
+        mixing[mine, :], profile[...], precision=lax.Precision.HIGHEST, preferred_element_type=F32
+    )
+
+    def gather_and_scatter(s, _):
+        gather(s, KB // 128)
+        scatter([s])
+        pack(s, s)
+        parcel_copy(s).start()
+        rate_of(s - ALONE, blocks - ALONE)
+        return 0
+
+    lax.fori_loop(ALONE, blocks, gather_and_scatter, 0)
     for q in range(KB // 128):
         moved[npar // 128 + q] = moved[q]
 
@@ -321,26 +379,19 @@
 
     lax.fori_loop(blocks, blocks + AHEAD, send, 0)
 
-    def wait_profile(k, _):
-        profile_copy(k).wait()
-        return 0
-
-    lax.fori_loop(1, n_span, wait_profile, 0)
-    for name in ("mixing", "nu", "gain", "advection"):
-        loads[name].wait()
-    corr = jnp.dot(
-        mixing[mine, :], profile[...], precision=lax.Precision.HIGHEST, preferred_element_type=F32
-    )
-    x = fields[0] + corr[:, 0:1]
-    rate = (jnp.maximum(x, 0.0) + jnp.log1p(jnp.exp(-jnp.abs(x)))) * (
-        1.0 + jnp.tanh(fields[1] + corr[:, 1:2])
-    )
-    source[0] = rate
-    for f in reversed(range(nf)):
+    def scatter_rest(t, _):
+        scatter([2 * t, 2 * t + 1])
+        for n in range(EACH):
+            send(blocks + AHEAD + EACH * t + n, 0)
+        return 0
+
+    lax.fori_loop(0, ALONE // 2, scatter_rest, 0)
+
+    for f in range(nf):
         deposit = jnp.concatenate(
             [total[f * A + q * rows : f * A + (q + 1) * rows, :] for q in range(chunks)], axis=1
         )
-        source[f] = 0.25 * (cond_gain[f] * rate - 0.5 * corr[:, f : f + 1] + deposit)
+        source[f] = 0.25 * (cond_gain[f] * rate[...] - 0.5 * corr[:, f : f + 1] + deposit)
 
     row_id = lax.broadcasted_iota(jnp.int32, (rows, cols), 0)
     col_id = lax.broadcasted_iota(jnp.int32, (rows, cols), 1)
@@ -382,7 +433,7 @@
     second_halo = halo_copies(1)
     for copy in second_halo:
         copy.start()
-    lax.fori_loop(blocks + AHEAD, n_pitch, send, 0)
+    lax.fori_loop(blocks + AHEAD + EACH * (ALONE // 2), n_pitch, send, 0)
     pack(n_pitch, 0)
     own_copy = pltpu.make_async_copy(outgoing.at[0], arrived.at[:, own_slots], own_sem)
     own_copy.start()
@@ -465,6 +516,9 @@
             dma((npar // KB,)),
             pltpu.SMEM((n_pitch,), jnp.int32),
             pltpu.VMEM((rows * cols // 16, 128), F32),
+            pltpu.VMEM((nf * A, 2 * B), BF),
+            pltpu.VMEM((rows, 128), F32),
+            pltpu.VMEM((rows, cols), F32),
             pltpu.VMEM((2, npar // 128, 128), jnp.int32),
             pltpu.SMEM((2, npar // 128, 128), jnp.int32),
             dma,

time: 50.1 us -> 47.4 us (0.946)
  Pallas kernels: 49.3 us -> 46.6 us
    pallas_call x1, Pallas kernels: 46.4 us -> 43.7 us  [local(): pl.pallas_call(functools.partial(step_kernel, n_pitch, n_span, cap), out_...]
where the time goes in v4:
time: 47.4 us; the launch traced here: 47.3 us
  Pallas kernels  46.6 us (98%)
  between operations  0.64 us (1%)
    pallas_call x1, Pallas kernels, local(): pl.pallas_call(functools.partial(step_kernel, n_pitch, n_span, cap), out_...  43.7 us
    pallas_call x1, Pallas kernels, local(): pl.pallas_call(hand_over_kernel, out_shape=tuple((jax.ShapeDtypeStruct(x....  2.89 us

profile of v4, /device:TPU:1, one launch (start us, length us, event | category | flops | bytes accessed | tf_op | source)
XLA Modules:
  0.0 47.3 jit_solution(15359976100540759635)
XLA Ops:
  0.6 43.7 %shard_map.122 = (f32[5,32,2048]{2,1,0:T(8,128)}, f32[16,16384]{1,0:T(8,128)}) custom-call(s32[32]{0:T(128)} %counts_hbm.1, f32[5]{0:T(128)} %gain_hbm.1, f32[2,5]{1,0:T(2,128)} %bitcast.6, s32[16,4,128]{2,1,0:T(4,128)} %bitcast.4, f32[5,32,2048]{2,1,0:T(8,128)} %fields_hbm.1, f32[32,2048]{1,0:T(8,128)} %nu_hbm.1, f32[256,256]{1,0:T(8,128)} %mixing_hbm.1, ...), custom_call_target="tpu_custom_call" | custom-call | flops 21474836480 | bytes 6291456 | tf_op jit(solution)/shard_map/pallas_call | solution.py:496
  44.4 2.9 %shard_map.123 = (f32[5,32,2048]{2,1,0:T(8,128)}, f32[16,16384]{1,0:T(8,128)}) custom-call(f32[5,32,2048]{2,1,0:T(8,128)} %get-tuple-element.4.fields_from, f32[16,16384]{1,0:T(8,128)} %get-tuple-element.5.arrived_from), custom_call_target="tpu_custom_call" | custom-call | tf_op jit(solution)/shard_map/pallas_call | solution.py:564

commit v5 on v4

--- a/solution.py
+++ b/solution.py
@@ -570,7 +570,7 @@
             pltpu.VMEM(results[0].shape, F32),
             pltpu.VMEM(results[1].shape, F32),
             dma((2, nf)),
-            dma((2, 8)),
+            dma((2, 4)),
         ],
         compiler_params=pltpu.CompilerParams(vmem_limit_bytes=60 << 20),
     )(*results)

time: 47.4 us -> 47.3 us (level)
  no operation moved by 1% of the time
where the time goes in v5:
time: 47.3 us; the launch traced here: 47.1 us
  Pallas kernels  46.5 us (98%)
  between operations  0.64 us (1%)
    pallas_call x1, Pallas kernels, local(): pl.pallas_call(functools.partial(step_kernel, n_pitch, n_span, cap), out_...  43.8 us
    pallas_call x1, Pallas kernels, local(): pl.pallas_call(hand_over_kernel, out_shape=tuple((jax.ShapeDtypeStruct(x....  2.71 us

profile of v5, /device:TPU:1, one launch (start us, length us, event | category | flops | bytes accessed | tf_op | source)
XLA Modules:
  0.0 47.1 jit_solution(9640334610699870092)
XLA Ops:
  0.6 43.8 %shard_map.122 = (f32[5,32,2048]{2,1,0:T(8,128)}, f32[16,16384]{1,0:T(8,128)}) custom-call(s32[32]{0:T(128)} %counts_hbm.1, f32[5]{0:T(128)} %gain_hbm.1, f32[2,5]{1,0:T(2,128)} %bitcast.6, s32[16,4,128]{2,1,0:T(4,128)} %bitcast.4, f32[5,32,2048]{2,1,0:T(8,128)} %fields_hbm.1, f32[32,2048]{1,0:T(8,128)} %nu_hbm.1, f32[256,256]{1,0:T(8,128)} %mixing_hbm.1, ...), custom_call_target="tpu_custom_call" | custom-call | flops 21474836480 | bytes 6291456 | tf_op jit(solution)/shard_map/pallas_call | solution.py:496
  44.4 2.7 %shard_map.123 = (f32[5,32,2048]{2,1,0:T(8,128)}, f32[16,16384]{1,0:T(8,128)}) custom-call(f32[5,32,2048]{2,1,0:T(8,128)} %get-tuple-element.4.fields_from, f32[16,16384]{1,0:T(8,128)} %get-tuple-element.5.arrived_from), custom_call_target="tpu_custom_call" | custom-call | tf_op jit(solution)/shard_map/pallas_call | solution.py:564
